TPU v7x, 32 devices: a whole 2x2x4 slice. The times are simulated.
32 devices in a mesh: gx: 2 (over core), gy: 4 (over y, x), gz: 4 (over z).
Axes of the slice: x: 2, y: 2, z: 4, core: 2. Of those that a mesh axis runs over, the one named last changes fastest.
Arguments:
- edge_state: bfloat16 [65536, 512], P(('gx', 'gy', 'gz')), may hold values from -6 to 6
- angle_weight: float32 [65536, 32], P(('gx', 'gy', 'gz')), may hold values from -6 to 6
- angle_bins: int32 [65536, 32], P(('gx', 'gy', 'gz')), may hold values from 0 to 15
- send_slots: int32 [2, 4, 4, 27, 32], P('gx', 'gy', 'gz'), may hold values from -1 to 2047, as said below
- fetch_index: int32 [65536], P(('gx', 'gy', 'gz')), may hold values from -1 to 2911, as said below
- down_weight: bfloat16 [2, 512, 64], replicated, may hold values from -0.25 to 0.25
- bilinear: bfloat16 [2, 1024, 64], replicated, may hold values from -0.1875 to 0.1875
- up_weight: bfloat16 [2, 64, 512], replicated, may hold values from -0.75 to 0.75
- first_dense: bfloat16 [2, 512, 512], replicated, may hold values from -0.25 to 0.25
- second_dense: bfloat16 [2, 512, 512], replicated, may hold values from -0.25 to 0.25
Outputs:
- edge_out: bfloat16 [65536, 512], P(('gx', 'gy', 'gz'))
Inputs may be any that keep to these rules, and one draw needn't show every extreme that they name: `send_slots`: direction t = 9a + 3b + c stands for the neighbouring brick at offset (a - 1, b - 1, c - 1), periodic. Row t of a brick lists, in its first slots, local edges whose reverses lie in the brick at direction t; the rest hold -1; row 13 holds only -1. Every edge is listed at most once. Some direction of every brick is full. `fetch_index`: -1 marks an empty neighbour slot. A value below 2048 is the local edge that is the reverse; 2048 + t * 32 + r says that the reverse is listed in slot r of row 26 - t of send_slots of the brick at direction t, and that this brick's own edge is listed in slot r of row t of its own send_slots. Reverses are mutual, live edges have live reverses, and rev of an edge is another edge.
All inputs are finite; a program needn't handle non-finite values.
Results may differ from a plain program's by a relative error of at most 0.014.
Values may be sent and summed in bfloat16 or wider, within the bound.
A program may use at most 128 MiB of HBM per device.

v0:
```python
import functools

import jax
import jax.numpy as jnp
from jax import lax
from jax.experimental import pallas as pl
from jax.experimental.pallas import tpu as pltpu
from jax.sharding import PartitionSpec as P

MESH = pl.DeviceIdType.MESH
HALF_ROOT = 0.7071067811865476
BF = jnp.bfloat16
F32 = jnp.float32
LANES = 128
CHUNK = 256


def silu(v):
    h = v * 0.5
    return h + h * jnp.tanh(h)


def place(t):
    if t < 13:
        return t, 0
    return (t - 18, 1) if t >= 18 else (t - 5, 1)


def dot(a, b):
    return jnp.dot(a, b, preferred_element_type=F32)


def kernel(
    sizes,
    rows_hbm,
    weight_hbm,
    bins_hbm,
    send_hbm,
    fetch_hbm,
    down_hbm,
    bilinear_hbm,
    up_hbm,
    first_hbm,
    second_hbm,
    out_hbm,
    rows,
    weight_in,
    bins_in,
    send_in,
    fetch_in,
    down_in,
    bilinear_in,
    up_in,
    first,
    second,
    down2,
    wide,
    up4,
    pick,
    pick_mask,
    send_pick,
    send_mask,
    live,
    nearby,
    coef,
    twice,
    table,
    packed,
    lifted_h,
    send_buf,
    recv_buf,
    in_sem,
    out_sem,
    send_sem,
    recv_sem,
):
    bx, by, bz, trip, slots = sizes
    edges, width = rows.shape
    quarter = edges // 4
    half_slots = slots // 2
    neigh = weight_in.shape[0]
    blocks = down_in.shape[0]
    angular = bilinear_in.shape[2] // trip
    pairs = angular // 2
    shift_quarter = quarter.bit_length() - 1
    shift_slots = slots.bit_length() - 1
    me = (lax.axis_index("gx"), lax.axis_index("gy"), lax.axis_index("gz"))

    loads = []
    for source, target in (
        (send_hbm, send_in),
        (fetch_hbm, fetch_in),
        (down_hbm, down_in),
        (rows_hbm, rows),
        (weight_hbm, weight_in),
        (bins_hbm, bins_in),
        (bilinear_hbm, bilinear_in),
        (up_hbm, up_in),
        (first_hbm, first),
        (second_hbm, second),
    ):
        loads.append(pltpu.make_async_copy(source, target, in_sem.at[len(loads)]))
        loads[-1].start()

    def neighbour(t):
        a, b, c = t // 9 - 1, t // 3 % 3 - 1, t % 3 - 1
        return (
            lax.rem(me[0] + (a + bx), bx),
            lax.rem(me[1] + (b + by), by),
            lax.rem(me[2] + (c + bz), bz),
        )

    parcels = []
    for t in range(27):
        if t == 13:
            continue
        block, half = place(26 - t)
        if bx == 2 and t // 9 != 1:
            if t < 9:
                parcels.append((t, block, 0, 2 * LANES))
        else:
            parcels.append((t, block, half * LANES, LANES))

    barrier = pltpu.get_barrier_semaphore()
    for t, _, _, _ in parcels:
        pl.semaphore_signal(barrier, inc=1, device_id=neighbour(t), device_id_type=MESH)

    lane = lax.broadcasted_iota(jnp.int32, (LANES, LANES), 1)
    sub = lax.broadcasted_iota(jnp.int32, (LANES, LANES), 0)

    def column(ref, i):
        return jnp.broadcast_to(ref[pl.ds(i, 1), :], (LANES, LANES)).T

    def ones_where(mask):
        return jnp.where(mask, F32(1), F32(0)).astype(BF)

    loads[0].wait()
    for i in range(send_pick.shape[0] // LANES):
        at = pl.ds(i * LANES, LANES)
        s = column(send_in, i)
        q = lax.shift_right_arithmetic(s, shift_quarter)
        k = jnp.where(s >= 0, s - q * quarter, -1)
        for m in range(quarter // LANES):
            send_pick[at, pl.ds(m * LANES, LANES)] = ones_where(k == lane + m * LANES)
        for m in range(2):
            send_mask[at, pl.ds(m * LANES, LANES)] = ones_where(
                q == 2 * m + lax.shift_right_logical(lane, 6)
            )
    low = lax.broadcasted_iota(jnp.int32, (half_slots, LANES), 1) < trip
    tail = recv_buf.shape[1] - 13 * half_slots
    for x in range(2 * blocks):
        recv_buf[x, pl.ds(13 * half_slots, tail), :] = jnp.zeros((tail, 2 * LANES), BF)

    loads[2].wait()
    for l in range(blocks):
        turned = down_in[l].astype(F32)
        down2[l] = jnp.concatenate([turned, turned], axis=0).T.astype(BF)
    loads[3].wait()

    def project(l, data):
        return silu(dot(data, down2[l])).astype(BF)

    def each_chunk(body):
        def run(i, carry):
            body(pl.multiple_of(i * CHUNK, CHUNK), i)
            return carry

        lax.fori_loop(0, edges // CHUNK, run, 0)

    def start_exchange(x):
        first_half = lax.broadcasted_iota(jnp.int32, (1, LANES), 1) < trip
        keep_low = ones_where(first_half)
        keep_high = ones_where(jnp.logical_not(first_half))
        for m in range(2):
            table[:, pl.ds(m * LANES, LANES)] = (
                twice[pl.ds(2 * m * quarter, quarter), :] * keep_low
                + twice[pl.ds((2 * m + 1) * quarter, quarter), :] * keep_high
            )
        for i in range(send_pick.shape[0] // LANES):
            at = pl.ds(i * LANES, LANES)
            found = dot(send_pick[at, :], table[...]).astype(BF) * send_mask[at, :]
            folded = found[:, :LANES].astype(F32) + found[:, LANES:].astype(F32)
            packed[at, :] = folded + pltpu.roll(folded, trip, 1)
        for t in range(27):
            if t == 13:
                continue
            block, half = place(26 - t)
            send_buf[x, pl.ds(block * half_slots, half_slots), pl.ds(half * LANES, LANES)] = jnp.where(
                low,
                packed[pl.ds(t * slots, half_slots), :],
                packed[pl.ds(t * slots + half_slots, half_slots), :],
            ).astype(BF)
        if x == 0:
            pl.semaphore_wait(barrier, len(parcels))
        copies = []
        for i, (t, block, at, count) in enumerate(parcels):
            where = (x, pl.ds(block * half_slots, half_slots), pl.ds(at, count))
            copies.append(
                pltpu.make_async_remote_copy(
                    src_ref=send_buf.at[where],
                    dst_ref=recv_buf.at[where],
                    send_sem=send_sem.at[x, i],
                    recv_sem=recv_sem.at[x, i],
                    device_id=neighbour(t),
                    device_id_type=MESH,
                )
            )
            copies[-1].start()
        return copies

    def find_nearby():
        def body(at, i):
            nearby[pl.ds(at, CHUNK), :] = dot(
                pick[pl.ds(at, CHUNK), pl.ds(0, quarter)], table[...]
            ).astype(BF)

        each_chunk(body)

    def reverse_rows(x, at):
        here = pl.ds(at, CHUNK)
        far = dot(pick[here, pl.ds(quarter, 2 * LANES)], recv_buf[x]).astype(BF)
        return (nearby[here, :] + far) * pick_mask[here, :]

    def prepare():
        loads[1].wait()
        loads[4].wait()
        loads[5].wait()

        def body(i, carry):
            at = pl.multiple_of(i * LANES, LANES)
            here = pl.ds(at, LANES)
            f = column(fetch_in, i)
            g = f - edges
            far = g >= 0
            t = lax.shift_right_arithmetic(g, shift_slots)
            r = g - t * slots
            upper = (t > 13).astype(jnp.int32)
            block = t - upper * jnp.where(t >= 18, 18, 5)
            side = lax.shift_right_arithmetic(r, shift_slots - 1)
            q_near = lax.shift_right_arithmetic(f, shift_quarter)
            k_far = quarter + block * half_slots + r - side * half_slots
            q = jnp.where(far, 2 * upper + side, q_near)
            k = jnp.where(far, k_far, jnp.where(f >= 0, f - q_near * quarter, -1))
            for m in range(pick.shape[1] // LANES):
                pick[here, pl.ds(m * LANES, LANES)] = ones_where(k == lane + m * LANES)
            for m in range(2):
                pick_mask[here, pl.ds(m * LANES, LANES)] = ones_where(
                    q == 2 * m + lax.shift_right_logical(lane, 6)
                )
            live[here, :] = jnp.where(f >= 0, F32(1), F32(0))
            copies = LANES // neigh
            w = weight_in[:, here]
            w = jnp.concatenate([w] * copies, axis=0).T
            n = bins_in[:, here]
            n = jnp.concatenate([n] * copies, axis=0).T
            own = (lane & (neigh - 1)) == (sub & (neigh - 1))
            w = jnp.where(own, F32(0), w)
            group = lax.shift_right_logical(lane, neigh.bit_length() - 1)
            for parity in range(2):
                for m in range(pairs // copies):
                    value = jnp.where(n == 2 * (m * copies + group) + parity, w, F32(0)).astype(BF)
                    for a in range(copies):
                        coef[
                            i * copies + a, pl.ds(parity * neigh, neigh), pl.ds(m * LANES, LANES)
                        ] = value[a * neigh : (a + 1) * neigh, :]
            return carry

        lax.fori_loop(0, edges // LANES, body, 0)
        loads[6].wait()
        loads[7].wait()
        for l in range(blocks):
            for p in range(pairs):
                turned = bilinear_in[l, :, pl.ds(p * LANES, LANES)].astype(F32).T
                both = jnp.concatenate([turned[:trip], turned[trip:]], axis=1).astype(BF)
                for q in range(4):
                    wide[l, pl.ds(q * trip, trip), pl.ds(p * LANES, LANES)] = both
            for q in range(4):
                up4[l, pl.ds(q * trip, trip), :] = up_in[l]

    first_lanes = lax.broadcasted_iota(jnp.int32, (neigh, LANES), 1) < trip

    def triplets(l, x):
        def body(at, i):
            lifted_h[...] = dot(reverse_rows(x, at), wide[l]).astype(BF)
            atoms = CHUNK // neigh
            for a in range(atoms):
                stacked = jnp.concatenate(
                    [lifted_h[pl.ds(a * neigh, neigh), pl.ds(p * LANES, LANES)] for p in range(pairs)],
                    axis=0,
                )
                both = dot(coef[i * atoms + a], stacked)
                chosen = jnp.where(first_lanes, both[:neigh], both[neigh:])
                twice[pl.ds(at + a * neigh, neigh), :] = (
                    chosen + pltpu.roll(chosen, trip, 1)
                ).astype(BF)

        each_chunk(body)

    def residual(l, x):
        def body(at, i):
            here = pl.ds(at, CHUNK)
            lifted = silu(dot(reverse_rows(x, at), up4[l])).astype(BF)
            mixed = ((rows[here, :].astype(F32) + lifted.astype(F32)) * HALF_ROOT).astype(BF)
            inner = silu(dot(mixed, first[l])).astype(BF)
            updated = (mixed.astype(F32) + silu(dot(inner, second[l]))) * HALF_ROOT
            alive = jnp.concatenate([live[here, :]] * (width // LANES), axis=1)
            done = jnp.where(alive > 0, updated, F32(0)).astype(BF)
            rows[here, :] = done
            if l + 1 < blocks:
                twice[here, :] = project(l + 1, done)
            else:
                pltpu.make_async_copy(rows.at[here], out_hbm.at[here], out_sem.at[i]).start()

        each_chunk(body)

    def first_project(at, i):
        twice[pl.ds(at, CHUNK), :] = project(0, rows[pl.ds(at, CHUNK), :])

    each_chunk(first_project)
    for l in range(blocks):
        copies = start_exchange(2 * l)
        if l == 0:
            prepare()
        find_nearby()
        for copy in copies:
            copy.wait()
        triplets(l, 2 * l)
        copies = start_exchange(2 * l + 1)
        find_nearby()
        if l == 0:
            loads[8].wait()
            loads[9].wait()
        for copy in copies:
            copy.wait()
        residual(l, 2 * l + 1)

    def finish(at, i):
        here = pl.ds(at, CHUNK)
        pltpu.make_async_copy(rows.at[here], out_hbm.at[here], out_sem.at[i]).wait()

    each_chunk(finish)


def solution(mesh):
    shape = mesh.shape

    def local(
        edge_state,
        angle_weight,
        angle_bins,
        send_slots,
        fetch_index,
        down_weight,
        bilinear,
        up_weight,
        first_dense,
        second_dense,
    ):
        edges, width = edge_state.shape
        neigh = angle_weight.shape[1]
        blocks, _, trip = down_weight.shape
        angular = bilinear.shape[1] // trip
        slots = send_slots.shape[-1]
        quarter = edges // 4
        senders = -(-27 * slots // LANES) * LANES
        listed = jnp.pad(
            send_slots.reshape(27 * slots), (0, senders - 27 * slots), constant_values=-1
        ).reshape(senders // LANES, LANES)
        depth = 2 * LANES
        sizes = (shape["gx"], shape["gy"], shape["gz"], trip, slots)
        parcels = 17 if shape["gx"] == 2 else 26
        exchange = pltpu.VMEM((2 * blocks, depth, 2 * LANES), BF)
        return pl.pallas_call(
            functools.partial(kernel, sizes),
            out_shape=jax.ShapeDtypeStruct((edges, width), BF),
            in_specs=[pl.BlockSpec(memory_space=pl.ANY)] * 10,
            out_specs=pl.BlockSpec(memory_space=pl.ANY),
            scratch_shapes=[
                pltpu.VMEM((edges, width), BF),
                pltpu.VMEM((neigh, edges), F32),
                pltpu.VMEM((neigh, edges), jnp.int32),
                pltpu.VMEM((senders // LANES, LANES), jnp.int32),
                pltpu.VMEM((edges // LANES, LANES), jnp.int32),
                pltpu.VMEM((blocks, trip, width), BF),
                pltpu.VMEM((blocks, trip, angular * trip), BF),
                pltpu.VMEM((blocks, trip, width), BF),
                pltpu.VMEM((blocks, width, width), BF),
                pltpu.VMEM((blocks, width, width), BF),
                pltpu.VMEM((blocks, width, LANES), BF),
                pltpu.VMEM((blocks, 4 * trip, angular * trip), BF),
                pltpu.VMEM((blocks, 4 * trip, width), BF),
                pltpu.VMEM((edges, quarter + depth), BF),
                pltpu.VMEM((edges, 2 * LANES), BF),
                pltpu.VMEM((senders, quarter), BF),
                pltpu.VMEM((senders, 2 * LANES), BF),
                pltpu.VMEM((edges, LANES), F32),
                pltpu.VMEM((edges, 2 * LANES), BF),
                pltpu.VMEM((edges // neigh, 2 * neigh, angular // 2 * neigh), BF),
                pltpu.VMEM((edges, LANES), BF),
                pltpu.VMEM((quarter, 2 * LANES), BF),
                pltpu.VMEM((senders, LANES), F32),
                pltpu.VMEM((CHUNK, angular * trip), BF),
                exchange,
                exchange,
                pltpu.SemaphoreType.DMA((10,)),
                pltpu.SemaphoreType.DMA((edges // CHUNK,)),
                pltpu.SemaphoreType.DMA((2 * blocks, parcels)),
                pltpu.SemaphoreType.DMA((2 * blocks, parcels)),
            ],
            compiler_params=pltpu.CompilerParams(
                collective_id=0, has_side_effects=True, vmem_limit_bytes=48 * 1024 * 1024
            ),
        )(
            edge_state,
            angle_weight.T,
            angle_bins.T,
            listed,
            fetch_index.reshape(edges // LANES, LANES),
            jnp.swapaxes(down_weight, 1, 2),
            jnp.swapaxes(bilinear, 1, 2),
            up_weight,
            first_dense,
            second_dense,
        )

    in_specs = (
        P(("gx", "gy", "gz"), None),
        P(("gx", "gy", "gz"), None),
        P(("gx", "gy", "gz"), None),
        P("gx", "gy", "gz", None, None),
        P(("gx", "gy", "gz")),
        P(),
        P(),
        P(),
        P(),
        P(),
    )
    out_specs = P(("gx", "gy", "gz"), None)
    return jax.shard_map(local, mesh=mesh, in_specs=in_specs, out_specs=out_specs, check_vma=False)
```

profile of v0, /device:TPU:0, one launch (start us, length us, event | category | flops | bytes accessed | tf_op | source)
XLA Modules:
  0.0 72.0 jit_solution(3111014559948652296)
XLA Ops:
  0.0 0.8 %reduce = s32[27,32]{1,0:T(8,128)S(1)} reduce(s32[1,1,1,27,32]{4,2,3,1,0:T(1,128)} %param.13, s32[]{:T(128)} %constant.5), dimensions={0,1,2}, to_apply=%param.13.reduce_sub_computation | reduce | bytes 6916 | tf_op args[3]
  0.8 0.1 reshape.9
  0.8 0.0 copy-start
  0.8 1.2 %copy-done = bf16[2,512,512]{2,1,0:T(8,128)(2,1)S(1)} copy-done((bf16[2,512,512]{2,1,0:T(8,128)(2,1)S(1)}, bf16[2,512,512]{2,1,0:T(8,128)(2,1)}, u32[]{:S(2)}) %copy-start) | copy-done | bytes 1048600
  2.1 0.0 copy-start.1
  2.1 1.2 %copy-done.1 = bf16[2,512,512]{2,1,0:T(8,128)(2,1)S(1)} copy-done((bf16[2,512,512]{2,1,0:T(8,128)(2,1)S(1)}, bf16[2,512,512]{2,1,0:T(8,128)(2,1)}, u32[]{:S(2)}) %copy-start.1) | copy-done | bytes 1048600
  3.3 0.0 copy-start.2
  3.3 0.9 %copy-done.2 = f32[2048,32]{0,1:T(8,128)S(1)} copy-done((f32[2048,32]{0,1:T(8,128)S(1)}, f32[2048,32]{0,1:T(8,128)}, u32[]{:S(2)}) %copy-start.2) | copy-done | bytes 262168
  4.2 0.0 copy-start.3
  4.2 0.9 %copy-done.3 = s32[2048,32]{0,1:T(8,128)S(1)} copy-done((s32[2048,32]{0,1:T(8,128)S(1)}, s32[2048,32]{0,1:T(8,128)}, u32[]{:S(2)}) %copy-start.3) | copy-done | bytes 262168
  5.2 0.0 copy-start.4
  5.2 0.9 %copy-done.4 = bf16[2,1024,64]{1,2,0:T(8,128)(2,1)S(1)} copy-done((bf16[2,1024,64]{1,2,0:T(8,128)(2,1)S(1)}, bf16[2,1024,64]{1,2,0:T(8,128)(2,1)}, u32[]{:S(2)}) %copy-start.4) | copy-done | bytes 262168
  6.1 0.0 copy-start.5
  6.1 0.9 %copy-done.5 = bf16[2,512,64]{1,2,0:T(8,128)(2,1)S(1)} copy-done((bf16[2,512,64]{1,2,0:T(8,128)(2,1)S(1)}, bf16[2,512,64]{1,2,0:T(8,128)(2,1)}, u32[]{:S(2)}) %copy-start.5) | copy-done | bytes 131096
  7.0 0.0 copy-start.6
  7.0 0.9 %copy-done.6 = bf16[2,64,512]{2,1,0:T(8,128)(2,1)S(1)} copy-done((bf16[2,64,512]{2,1,0:T(8,128)(2,1)S(1)}, bf16[2,64,512]{2,1,0:T(8,128)(2,1)}, u32[]{:S(2)}) %copy-start.6) | copy-done | bytes 131096
  7.9 0.0 copy-start.7
  8.0 0.7 copy-done.7
  8.6 62.0 %shard_map.100 = bf16[2048,512]{1,0:T(8,128)(2,1)S(1)} custom-call(bf16[2048,512]{1,0:T(8,128)(2,1)} %rows_hbm.1, f32[32,2048]{1,0:T(8,128)S(1)} %bitcast.7, s32[32,2048]{1,0:T(8,128)S(1)} %bitcast.8, s32[7,128]{1,0:T(8,128)S(1)} %pad_bitcast_fusion.send_hbm, s32[16,128]{1,0:T(8,128)S(1)} %bitcast.11, bf16[2,64,512]{2,1,0:T(8,128)(2,1)S(1)} %bitcast.10, ...), custom_call_target="tpu_custom_call" | custom-call | tf_op jit(solution)/shard_map/pallas_call | solution.py:373
  70.6 1.3 %copy.12 = bf16[2048,512]{1,0:T(8,128)(2,1)} copy(bf16[2048,512]{1,0:T(8,128)(2,1)S(1)} %shard_map.100) | data formatting | bytes 4194304
  (1 shorter events, 0.0 us)
Async XLA Ops:
  0.8 1.2 %copy-start = (bf16[2,512,512]{2,1,0:T(8,128)(2,1)S(1)}, bf16[2,512,512]{2,1,0:T(8,128)(2,1)}, u32[]{:S(2)}) copy-start(bf16[2,512,512]{2,1,0:T(8,128)(2,1)} %first_hbm.1) | copy-start | bytes 3145732
  2.1 1.2 %copy-start.1 = (bf16[2,512,512]{2,1,0:T(8,128)(2,1)S(1)}, bf16[2,512,512]{2,1,0:T(8,128)(2,1)}, u32[]{:S(2)}) copy-start(bf16[2,512,512]{2,1,0:T(8,128)(2,1)} %second_hbm.1) | copy-start | bytes 3145732
  3.3 0.9 %copy-start.2 = (f32[2048,32]{0,1:T(8,128)S(1)}, f32[2048,32]{0,1:T(8,128)}, u32[]{:S(2)}) copy-start(f32[2048,32]{0,1:T(8,128)} %param.11) | copy-start | bytes 786436
  4.2 0.9 %copy-start.3 = (s32[2048,32]{0,1:T(8,128)S(1)}, s32[2048,32]{0,1:T(8,128)}, u32[]{:S(2)}) copy-start(s32[2048,32]{0,1:T(8,128)} %param.12) | copy-start | bytes 786436
  5.2 0.9 %copy-start.4 = (bf16[2,1024,64]{1,2,0:T(8,128)(2,1)S(1)}, bf16[2,1024,64]{1,2,0:T(8,128)(2,1)}, u32[]{:S(2)}) copy-start(bf16[2,1024,64]{1,2,0:T(8,128)(2,1)} %param.16) | copy-start | bytes 786436
  6.1 0.9 %copy-start.5 = (bf16[2,512,64]{1,2,0:T(8,128)(2,1)S(1)}, bf16[2,512,64]{1,2,0:T(8,128)(2,1)}, u32[]{:S(2)}) copy-start(bf16[2,512,64]{1,2,0:T(8,128)(2,1)} %param.15) | copy-start | bytes 393220
  7.0 0.9 %copy-start.6 = (bf16[2,64,512]{2,1,0:T(8,128)(2,1)S(1)}, bf16[2,64,512]{2,1,0:T(8,128)(2,1)}, u32[]{:S(2)}) copy-start(bf16[2,64,512]{2,1,0:T(8,128)(2,1)} %up_hbm.1) | copy-start | bytes 393220
  7.9 0.7 copy-start.7
where the time goes:
time: 72.4 us; the launch traced here: 72 us
  Pallas kernels  62 us (86%)
  local copies, waits for them, and re-layouts  9.2 us (13%)
  other arithmetic  0.75 us (1%)
    pallas_call x1, Pallas kernels, local(): pl.pallas_call(functools.partial(kernel, sizes), out_shape=jax.ShapeDtype...  62 us
    unnamed x17, local copies, waits for them, and re-layouts  9.12 us

commit v1 on v0

--- a/solution.py
+++ b/solution.py
@@ -12,11 +12,11 @@
 BF = jnp.bfloat16
 F32 = jnp.float32
 LANES = 128
-CHUNK = 256
+CHUNK = 1024
 
 
 def silu(v):
-    h = v * 0.5
+    h = v.astype(BF) * BF(0.5)
     return h + h * jnp.tanh(h)
 
 
@@ -158,7 +158,7 @@
     loads[3].wait()
 
     def project(l, data):
-        return silu(dot(data, down2[l])).astype(BF)
+        return silu(dot(data, down2[l]))
 
     def each_chunk(body):
         def run(i, carry):
@@ -299,10 +299,10 @@
     def residual(l, x):
         def body(at, i):
             here = pl.ds(at, CHUNK)
-            lifted = silu(dot(reverse_rows(x, at), up4[l])).astype(BF)
+            lifted = silu(dot(reverse_rows(x, at), up4[l]))
             mixed = ((rows[here, :].astype(F32) + lifted.astype(F32)) * HALF_ROOT).astype(BF)
-            inner = silu(dot(mixed, first[l])).astype(BF)
-            updated = (mixed.astype(F32) + silu(dot(inner, second[l]))) * HALF_ROOT
+            inner = silu(dot(mixed, first[l]))
+            updated = (mixed.astype(F32) + silu(dot(inner, second[l])).astype(F32)) * HALF_ROOT
             alive = jnp.concatenate([live[here, :]] * (width // LANES), axis=1)
             done = jnp.where(alive > 0, updated, F32(0)).astype(BF)
             rows[here, :] = done
@@ -408,7 +408,7 @@
                 pltpu.SemaphoreType.DMA((2 * blocks, parcels)),
             ],
             compiler_params=pltpu.CompilerParams(
-                collective_id=0, has_side_effects=True, vmem_limit_bytes=48 * 1024 * 1024
+                collective_id=0, has_side_effects=True, vmem_limit_bytes=60 * 1024 * 1024
             ),
         )(
             edge_state,

time: 72.4 us -> 50.8 us (0.70)
  Pallas kernels: 62 us -> 46.1 us
  local copies, waits for them, and re-layouts: 9.2 us -> 3.72 us
    pallas_call x1, Pallas kernels: 62 us -> 46.1 us  [local(): pl.pallas_call(functools.partial(kernel, sizes), out_shape=jax.ShapeDtype...]
    unnamed x17 -> x1, local copies, waits for them, and re-layouts: 9.12 us -> 3.05 us
where the time goes in v1:
time: 50.8 us; the launch traced here: 50.6 us
  Pallas kernels  46.1 us (91%)
  local copies, waits for them, and re-layouts  3.72 us (7%)
  other arithmetic  0.75 us (1%)
    pallas_call x1, Pallas kernels, local(): pl.pallas_call(functools.partial(kernel, sizes), out_shape=jax.ShapeDtype...  46.1 us
    unnamed x1, local copies, waits for them, and re-layouts  3.05 us

profile of v1, /device:TPU:0, one launch (start us, length us, event | category | flops | bytes accessed | tf_op | source)
XLA Modules:
  0.0 50.6 jit_solution(7355845429936275409)
XLA Ops:
  0.0 0.8 %reduce = s32[27,32]{1,0:T(8,128)S(1)} reduce(s32[1,1,1,27,32]{4,2,3,1,0:T(1,128)} %param.13, s32[]{:T(128)} %constant.5), dimensions={0,1,2}, to_apply=%param.13.reduce_sub_computation | reduce | bytes 6916 | tf_op args[3]
  0.8 0.1 reshape.9
  0.8 0.6 %pad_bitcast_fusion.send_hbm = s32[7,128]{1,0:T(8,128)} fusion(s32[864]{0:T(1024)S(1)} %reshape.9), kind=kLoop, calls=%fused_computation | loop fusion | bytes 7040 | tf_op jit(solution)/shard_map/reshape | solution.py:368
  1.4 46.1 %shard_map.100 = bf16[2048,512]{1,0:T(8,128)(2,1)} custom-call(bf16[2048,512]{1,0:T(8,128)(2,1)} %rows_hbm.1, f32[32,2048]{1,0:T(8,128)} %bitcast.7, s32[32,2048]{1,0:T(8,128)} %bitcast.8, s32[7,128]{1,0:T(8,128)} %pad_bitcast_fusion.send_hbm, s32[16,128]{1,0:T(8,128)} %bitcast.11, bf16[2,64,512]{2,1,0:T(8,128)(2,1)} %bitcast.10, ...), custom_call_target="tpu_custom_call" | custom-call | tf_op jit(solution)/shard_map/pallas_call | solution.py:373
  47.5 3.0 %copy.12 = bf16[2048,512]{1,0:T(8,128)(2,1)} copy(bf16[2048,512]{1,0:T(8,128)(2,1)} %shard_map.100) | data formatting | bytes 4194304

commit v2 on v1

--- a/solution.py
+++ b/solution.py
@@ -176,11 +176,9 @@
                 twice[pl.ds(2 * m * quarter, quarter), :] * keep_low
                 + twice[pl.ds((2 * m + 1) * quarter, quarter), :] * keep_high
             )
-        for i in range(send_pick.shape[0] // LANES):
-            at = pl.ds(i * LANES, LANES)
-            found = dot(send_pick[at, :], table[...]).astype(BF) * send_mask[at, :]
-            folded = found[:, :LANES].astype(F32) + found[:, LANES:].astype(F32)
-            packed[at, :] = folded + pltpu.roll(folded, trip, 1)
+        found = dot(send_pick[...], table[...]).astype(BF) * send_mask[...]
+        folded = found[:, :LANES].astype(F32) + found[:, LANES:].astype(F32)
+        packed[...] = folded + pltpu.roll(folded, trip, 1)
         for t in range(27):
             if t == 13:
                 continue
@@ -265,7 +263,7 @@
                         ] = value[a * neigh : (a + 1) * neigh, :]
             return carry
 
-        lax.fori_loop(0, edges // LANES, body, 0)
+        lax.fori_loop(0, edges // LANES, body, 0, unroll=4)
         loads[6].wait()
         loads[7].wait()
         for l in range(blocks):

time: 50.8 us -> 50.5 us (level)
  no operation moved by 1% of the time
where the time goes in v2:
time: 50.5 us; the launch traced here: 50.3 us
  Pallas kernels  45.8 us (91%)
  local copies, waits for them, and re-layouts  3.72 us (7%)
  other arithmetic  0.75 us (1%)
    pallas_call x1, Pallas kernels, local(): pl.pallas_call(functools.partial(kernel, sizes), out_shape=jax.ShapeDtype...  45.8 us
    unnamed x1, local copies, waits for them, and re-layouts  3.05 us

profile of v2, /device:TPU:0, one launch (start us, length us, event | category | flops | bytes accessed | tf_op | source)
XLA Modules:
  0.0 50.3 jit_solution(4941562395729493477)
XLA Ops:
  0.0 0.8 %reduce = s32[27,32]{1,0:T(8,128)S(1)} reduce(s32[1,1,1,27,32]{4,2,3,1,0:T(1,128)} %param.13, s32[]{:T(128)} %constant.5), dimensions={0,1,2}, to_apply=%param.13.reduce_sub_computation | reduce | bytes 6916 | tf_op args[3]
  0.8 0.1 reshape.9
  0.8 0.6 %pad_bitcast_fusion.send_hbm = s32[7,128]{1,0:T(8,128)} fusion(s32[864]{0:T(1024)S(1)} %reshape.9), kind=kLoop, calls=%fused_computation | loop fusion | bytes 7040 | tf_op jit(solution)/shard_map/reshape | solution.py:366
  1.4 45.8 %shard_map.100 = bf16[2048,512]{1,0:T(8,128)(2,1)} custom-call(bf16[2048,512]{1,0:T(8,128)(2,1)} %rows_hbm.1, f32[32,2048]{1,0:T(8,128)} %bitcast.7, s32[32,2048]{1,0:T(8,128)} %bitcast.8, s32[7,128]{1,0:T(8,128)} %pad_bitcast_fusion.send_hbm, s32[16,128]{1,0:T(8,128)} %bitcast.11, bf16[2,64,512]{2,1,0:T(8,128)(2,1)} %bitcast.10, ...), custom_call_target="tpu_custom_call" | custom-call | tf_op jit(solution)/shard_map/pallas_call | solution.py:371
  47.2 3.0 %copy.12 = bf16[2048,512]{1,0:T(8,128)(2,1)} copy(bf16[2048,512]{1,0:T(8,128)(2,1)} %shard_map.100) | data formatting | bytes 4194304
